TPU v7x, 256 devices: a whole 4x4x8 slice. The times are simulated.
256 devices in a mesh: expert: 16 (over x_hi, y, core), dp: 16 (over x_lo, z).
Axes of the slice: x: 4 (x_hi: 2, x_lo: 2; x = x_hi * 2 + x_lo), y: 4, z: 8, core: 2. Of those that a mesh axis runs over, the one named last changes fastest.
Arguments:
- cotangent: bfloat16 [32768, 2048], P(('expert', 'dp')), may hold values from -6 to 6
- hidden: bfloat16 [32768, 7168], P(('expert', 'dp')), may hold values from -0.1796875 to 0.1796875
- codes: bfloat16 [16, 7168, 1024], P('expert', 'dp'), may hold values from -0.125 to 0.125
- scales: float32 [16, 7168], P('expert', 'dp'), may hold values from 0.3 to 3
- counts: int32 [256, 8], replicated, may hold values from 0 to 24, as said below
Outputs:
- d_hidden: bfloat16 [32768, 7168], P(('expert', 'dp'))
- weight_grad: float32 [16, 7168, 1024], P('expert', 'dp')
Inputs may be any that keep to these rules, and one draw needn't show every extreme that they name: Row p of counts is device p's split of its 128 rows over the experts, devices numbered with the expert index first; a device's rows are grouped by expert in increasing order. Each row sums to 128 and has an entry equal to 24. In every draw all devices of one pair of neighbouring expert indices give their 24 rows to the same expert.
All inputs are finite; a program needn't handle non-finite values.
Results may differ from a plain program's by a relative error of at most 0.001.
Values may be sent and summed in bfloat16 or wider, within the bound.
No kernel may reach another device: no remote copies, remote signals or barrier semaphores. Data moves between devices by JAX's collectives and lax.ppermute only.
A program may use at most 192 MiB of HBM per device.

v0:
```python
import jax
import jax.numpy as jnp
from jax import lax
from jax.experimental import pallas as pl
from jax.experimental.pallas import tpu as pltpu
from jax.sharding import Mesh, PartitionSpec as P

PLACES = ("xh", "y")
SWAP = [(0, 1), (1, 0)]


def slot_hot(row_counts, slots, rows):
    starts = jnp.cumsum(row_counts, axis=-1) - row_counts
    slot = jnp.arange(slots, dtype=jnp.int32)
    source = jnp.where(slot < row_counts[..., None], starts[..., None] + slot, -1)
    return (source[..., None] == jnp.arange(rows, dtype=jnp.int32)).astype(jnp.bfloat16)


def distances(depth):
    order = [depth // 2]
    for k in range(depth // 2 - 1, 0, -1):
        order += [k, -k]
    return order + [0]


def after(value, *others):
    return lax.optimization_barrier((value,) + others)[0]


def along_z(value, by):
    depth = lax.axis_size("z")
    return lax.ppermute(value, "z", [(i, (i + by) % depth) for i in range(depth)])


def split_kernel(level_ref, hidden_ref, *refs):
    outs, held = refs[:-1], refs[-1]
    depth, _, wide = held.shape
    share = wide // 2
    for z in range(depth):
        low = hidden_ref[:, z * share : (z + 1) * share]
        high = hidden_ref[:, (depth + z) * share : (depth + z + 1) * share]
        held[z] = jnp.concatenate([low, high], axis=1)
    for out, by in zip(outs, distances(depth)):
        out[...] = held[lax.rem(level_ref[0] + (by + depth), depth)]


def split_levels(hidden, level, depth):
    rows, width = hidden.shape
    block = (rows, width // depth)
    whole = pl.BlockSpec(memory_space=pltpu.VMEM)
    return pl.pallas_call(
        split_kernel,
        out_shape=[jax.ShapeDtypeStruct(block, hidden.dtype)] * depth,
        in_specs=[pl.BlockSpec(memory_space=pltpu.SMEM), whole],
        out_specs=[whole] * depth,
        scratch_shapes=[pltpu.VMEM((depth,) + block, hidden.dtype)],
        compiler_params=pltpu.CompilerParams(vmem_limit_bytes=40 << 20),
    )(level, hidden)


def join_kernel(level_ref, *refs):
    parts, out_ref, held = refs[:-2], refs[-2], refs[-1]
    depth, _, wide = held.shape
    share = wide // 2
    for part, by in zip(parts, distances(depth)):
        held[lax.rem(level_ref[0] + (by + depth), depth)] = part[...]
    for z in range(0, depth, 2):
        for s in range(2):
            pair = [held[z + i, :, s * share : (s + 1) * share] for i in range(2)]
            out_ref[:, (s * depth + z) * share : (s * depth + z + 2) * share] = (
                jnp.concatenate(pair, axis=1)
            )


def join_levels(parts, level):
    depth = len(parts)
    rows, wide = parts[0].shape
    whole = pl.BlockSpec(memory_space=pltpu.VMEM)
    return pl.pallas_call(
        join_kernel,
        out_shape=jax.ShapeDtypeStruct((rows, depth * wide), parts[0].dtype),
        in_specs=[pl.BlockSpec(memory_space=pltpu.SMEM)] + [whole] * depth,
        out_specs=whole,
        scratch_shapes=[pltpu.VMEM((depth, rows, wide), parts[0].dtype)],
        compiler_params=pltpu.CompilerParams(vmem_limit_bytes=40 << 20),
    )(level, *parts)


def pass_on(next_ref, passed_ref):
    for i in range(next_ref.shape[0]):
        passed_ref[i] = next_ref[i]


def mate_kernel(place_ref, core_ref, next_ref, codes_ref, scales_ref, *refs):
    rows_refs, out_ref, passed_ref = refs[:-2], refs[-2], refs[-1]
    pass_on(next_ref, passed_ref)
    values = jnp.concatenate([ref[0, 0] for ref in rows_refs])
    out_ref[...] = scales_ref[...] * jnp.dot(
        values, codes_ref[...], preferred_element_type=jnp.float32
    )


def own_kernel(place_ref, core_ref, next_ref, codes_ref, scales_ref, *refs):
    rows_refs, mate_ref, out_ref, passed_ref = refs[:-3], refs[-3], refs[-2], refs[-1]
    pass_on(next_ref, passed_ref)
    values = jnp.concatenate([ref[0, 0] for ref in rows_refs])
    total = mate_ref[...] + scales_ref[...] * jnp.dot(
        values, codes_ref[...], preferred_element_type=jnp.float32
    )
    places, steps, slots, wide = out_ref.shape
    total = total.reshape(steps, places, slots, wide).astype(out_ref.dtype)
    for step in range(steps):
        out_ref[:, step] = total[step]


def partials(where, core, then, values, codes, scales, mate=None, places=None):
    steps = where.shape[0]
    _, _, rows, half = values.shape
    wide = codes.shape[1]
    flip = 1 if mate is None else 0

    def rows_spec(j):
        return pl.BlockSpec((1, 1, rows, half), lambda i, w, c: (w[j], c[0] ^ flip, 0, 0))

    def whole(*shape):
        return pl.BlockSpec(shape, lambda i, w, c: (0,) * len(shape))

    words = pl.BlockSpec(memory_space=pltpu.SMEM)
    in_specs = [words, whole(half, wide), whole(1, wide)] + [rows_spec(j) for j in range(steps)]
    if mate is None:
        kernel, shape, dtype, extra = mate_kernel, (steps * rows, wide), jnp.float32, ()
    else:
        kernel, extra = own_kernel, (mate,)
        in_specs.append(whole(steps * rows, wide))
        shape, dtype = (places, steps, rows // places, wide), jnp.bfloat16
    return pl.pallas_call(
        kernel,
        out_shape=[jax.ShapeDtypeStruct(shape, dtype), jax.ShapeDtypeStruct(then.shape, then.dtype)],
        grid_spec=pltpu.PrefetchScalarGridSpec(
            num_scalar_prefetch=2, grid=(1,), in_specs=in_specs, out_specs=[whole(*shape), words]
        ),
        compiler_params=pltpu.CompilerParams(vmem_limit_bytes=40 << 20),
    )(where, core, then, codes, scales, *[values] * steps, *extra)


def weight_kernel(core_ref, values_ref, own_ref, mate_ref, out_ref):
    me = core_ref[0]
    levels = range(values_ref.shape[0])
    rows = [values_ref[z, me] for z in levels] + [values_ref[z, 1 - me] for z in levels]
    units = jnp.concatenate([own_ref[...], mate_ref[...]])
    part = lax.dot_general(
        units, jnp.concatenate(rows), (((0,), (0,)), ((), ())), preferred_element_type=jnp.float32
    )

    @pl.when(pl.program_id(0) == 0)
    def _():
        out_ref[...] = part

    @pl.when(pl.program_id(0) > 0)
    def _():
        out_ref[...] += part


def weight_sums(core, values, own, mate, levels=2):
    depth, _, rows, half = values.shape
    wide = own.shape[1]
    units = pl.BlockSpec((levels * rows, wide), lambda i, c: (i, 0))
    return pl.pallas_call(
        weight_kernel,
        out_shape=jax.ShapeDtypeStruct((wide, half), jnp.float32),
        grid_spec=pltpu.PrefetchScalarGridSpec(
            num_scalar_prefetch=1,
            grid=(depth // levels,),
            in_specs=[
                pl.BlockSpec((levels, 2, rows, half), lambda i, c: (i, 0, 0, 0)), units, units
            ],
            out_specs=pl.BlockSpec((wide, half), lambda i, c: (0, 0)),
        ),
        compiler_params=pltpu.CompilerParams(vmem_limit_bytes=40 << 20),
    )(core, values, own, mate)


def rows_kernel(counts_ref, rows_ref, out_ref):
    halves, experts, slots, half = out_ref.shape
    rows = rows_ref.shape[0]
    slot = lax.broadcasted_iota(jnp.int32, (slots, rows), 0)
    row = lax.broadcasted_iota(jnp.int32, (slots, rows), 1)
    hot, start = [], 0
    for e in range(experts):
        count = counts_ref[e]
        hit = jnp.logical_and(row == slot + start, slot < count)
        hot.append(jnp.where(hit, 1.0, 0.0))
        start = start + count
    hot = jnp.concatenate(hot).astype(jnp.bfloat16)
    for c in range(halves):
        packed = jnp.dot(
            hot, rows_ref[:, c * half : (c + 1) * half], preferred_element_type=jnp.float32
        )
        out_ref[c] = packed.reshape(experts, slots, half).astype(out_ref.dtype)


def pack_rows(counts, cotangent, slots):
    rows, cols = cotangent.shape
    whole = pl.BlockSpec(memory_space=pltpu.VMEM)
    return pl.pallas_call(
        rows_kernel,
        out_shape=jax.ShapeDtypeStruct((2, counts.shape[0], slots, cols // 2), cotangent.dtype),
        in_specs=[pl.BlockSpec(memory_space=pltpu.SMEM), whole],
        out_specs=whole,
        compiler_params=pltpu.CompilerParams(vmem_limit_bytes=40 << 20),
    )(counts, cotangent)


def unpack_kernel(hot_ref, back_ref, *outs):
    experts, _, slots, wide = back_ref.shape
    for i, out in enumerate(outs):
        packed = back_ref[:, i].astype(jnp.float32).reshape(experts * slots, wide)
        out[...] = lax.dot_general(
            hot_ref[i], packed.astype(jnp.bfloat16), (((0,), (0,)), ((), ())),
            preferred_element_type=jnp.float32,
        ).astype(out.dtype)


def unpack(hot, back):
    steps, _, rows = hot.shape
    whole = pl.BlockSpec(memory_space=pltpu.VMEM)
    return pl.pallas_call(
        unpack_kernel,
        out_shape=[jax.ShapeDtypeStruct((rows, back.shape[-1]), back.dtype)] * steps,
        in_specs=[whole, whole],
        out_specs=[whole] * steps,
        compiler_params=pltpu.CompilerParams(vmem_limit_bytes=40 << 20),
    )(hot, back)


def pack_kernel(level_ref, hot_ref, *refs):
    blocks, out_ref = refs[:-1], refs[-1]
    experts, depth, slots, wide = out_ref.shape
    for i, by in enumerate(distances(depth)):
        packed = jnp.dot(hot_ref[i], blocks[i][...], preferred_element_type=jnp.float32)
        level = lax.rem(level_ref[0] + (by + depth), depth)
        out_ref[:, level] = packed.reshape(experts, slots, wide).astype(out_ref.dtype)


def pack_hidden(hot, blocks, level, experts):
    depth, places, rows = hot.shape
    wide = blocks[0].shape[1]
    whole = pl.BlockSpec(memory_space=pltpu.VMEM)
    return pl.pallas_call(
        pack_kernel,
        out_shape=jax.ShapeDtypeStruct((experts, depth, places // experts, wide), jnp.bfloat16),
        in_specs=[pl.BlockSpec(memory_space=pltpu.SMEM)] + [whole] * (depth + 1),
        out_specs=whole,
        compiler_params=pltpu.CompilerParams(vmem_limit_bytes=40 << 20),
    )(level, hot, *blocks)


def shards(cotangent, hidden, codes, scales, counts):
    rows, cols = cotangent.shape
    half = cols // 2
    share = codes.shape[1]
    places = lax.axis_size(PLACES)
    depth = lax.axis_size("z")
    experts = counts.shape[1]
    slots = 3 * rows // (2 * experts)
    wide = 2 * share
    order = distances(depth)
    place, core = lax.axis_index(PLACES), lax.axis_index("c")
    side, level = lax.axis_index("xl"), lax.axis_index("z")
    core_word = core.astype(jnp.int32).reshape(1)
    level_word = level.astype(jnp.int32).reshape(1)

    def levels_at(steps):
        return (level.astype(jnp.int32) + jnp.array(steps, jnp.int32) + depth) % depth

    line_at = ((place * 2 + core) * 2 + side) * depth
    own_counts = lax.dynamic_slice_in_dim(counts, line_at + level, 1, 0).reshape(experts)
    line_counts = lax.dynamic_slice_in_dim(counts, line_at, depth, 0)
    near_counts = lax.dynamic_slice_in_dim(jnp.concatenate([line_counts] * 2), level, depth, 0)
    near_counts = jnp.stack([near_counts[by % depth] for by in order])
    near_hot = slot_hot(near_counts, slots, rows).reshape(depth, experts * slots, rows)

    other_codes, other_scales = lax.ppermute((codes[0], scales[0]), "xl", SWAP)
    by_level = split_levels(hidden, level_word, depth)

    packed = pack_rows(own_counts, cotangent, slots).reshape(2 * experts, slots, half)
    arrived = lax.all_to_all(packed, ("c",) + PLACES, 0, 0).reshape(2, places * slots, half)

    line_hidden = {}
    for block, by in zip(by_level, order):
        line_hidden[-by if by < depth // 2 else by] = along_z(block, by) if by else block
    arrived, line_hidden[-1], line_hidden[1] = lax.optimization_barrier(
        (arrived, line_hidden[-1], line_hidden[1])
    )
    values = lax.all_gather(arrived.reshape(2 * places * slots, half), "z", axis=0, tiled=True)
    values = values.reshape(depth, 2, places * slots, half)

    first = side == 0
    both_codes = jnp.where(first, jnp.stack([codes[0], other_codes]),
                           jnp.stack([other_codes, codes[0]])).reshape(wide, half).T
    both_scales = jnp.where(first, jnp.stack([scales[0], other_scales]),
                            jnp.stack([other_scales, scales[0]])).reshape(1, wide)
    both_codes, both_scales, *line_hidden = lax.optimization_barrier(
        [both_codes, both_scales] + [line_hidden[by] for by in order]
    )

    hidden_slots = pack_hidden(near_hot, line_hidden, level_word, experts)
    own_hidden = lax.all_to_all(hidden_slots, PLACES, 0, 0)
    own_hidden = own_hidden.transpose(1, 0, 2, 3).reshape(depth * places * slots, wide)
    mate_hidden = lax.ppermute(own_hidden, "c", SWAP)
    values = after(values, own_hidden)

    def product(where, then, *mate):
        args = (where, core_word, then, values, both_codes, both_scales)
        return partials(*args, *mate, places) if mate else partials(*args)

    came = {}

    def send_home(steps, back):
        for by, block in zip(steps, back):
            came[-by if by < depth // 2 else by] = along_z(block, by) if by else block

    cut = 3
    far_at, close_at = levels_at(order[:cut]), levels_at(order[cut:])
    far_mate, far_at = product(far_at, far_at)
    far_joined, close_at = product(far_at, close_at, lax.ppermute(far_mate, "c", SWAP))
    close_mate, close_at = product(close_at, close_at)
    close_joined, _ = product(close_at, far_at, lax.ppermute(close_mate, "c", SWAP))
    sums = weight_sums(core_word, values, own_hidden, mate_hidden)
    close_joined = after(close_joined, sums)
    far_raw = after(lax.all_to_all(far_joined, PLACES, 0, 0), close_joined, sums)
    send_home(order[:cut], unpack(near_hot[:cut], far_raw))
    close_raw = after(lax.all_to_all(close_joined, PLACES, 0, 0), *came.values())
    send_home(order[cut:], unpack(near_hot[cut:], close_raw))

    sums = sums.reshape(2, share, half)
    gone = lax.dynamic_index_in_dim(sums, 1 - side, 0, keepdims=False)
    kept = lax.dynamic_index_in_dim(sums, side, 0, keepdims=False)
    largest = jnp.maximum(jnp.max(jnp.abs(gone)), 1e-30).reshape(1)
    gone = (gone * (1 / largest)).astype(jnp.float16)
    largest = lax.ppermute(largest, "xl", SWAP)
    gone, kept, largest, _ = lax.optimization_barrier((gone, kept, largest, close_raw))
    gone = lax.ppermute(gone, "xl", SWAP)
    weight_grad = kept + gone.astype(jnp.float32) * largest
    d_hidden = join_levels([came[by] for by in order], after(level_word, weight_grad))
    return d_hidden, weight_grad[None]


def solution(mesh):
    lanes, lines = mesh.devices.shape
    fine = Mesh(mesh.devices.reshape(2, lanes // 4, 2, 2, lines // 2), ("xh", "y", "c", "xl", "z"))
    expert, dp = ("xh", "y", "c"), ("xl", "z")
    in_specs = (P(expert + dp, None), P(expert + dp, None), P(expert, dp, None), P(expert, dp), P())
    out_specs = (P(expert + dp, None), P(expert, dp, None))
    return jax.shard_map(shards, mesh=fine, in_specs=in_specs, out_specs=out_specs, check_vma=False)
```

profile of v0, /device:TPU:6, one launch (start us, length us, event | category | flops | bytes accessed | tf_op | source)
XLA Modules:
  0.0 255.7 jit_solution(1101682400530660512)
XLA Ops:
  7.2 0.7 copy-done
  7.9 0.2 dynamic-slice_reduce_fusion.counts_ref
  8.1 1.0 copy-done.9
  9.1 1.8 shard_map.86
  10.9 7.6 %all-to-all-start = ((bf16[16,24,1024]{2,1,0:T(8,128)(2,1)}), bf16[16,24,1024]{2,1,0:T(8,128)(2,1)}, u32[]{:S(2)}, u32[]{:S(2)}) async-start(bf16[16,24,1024]{2,1,0:T(8,128)(2,1)} %bitcast.2), calls=%async_computation | async-start | bytes 1572864 | tf_op jit(solution)/shard_map/all_to_all | solution.py:287
  18.5 1.2 shard_map.87
  19.7 0.7 copy-done.10
  20.4 0.7 copy-done.11
  21.1 1.9 collective-permute-start
  23.0 3.9 %collective-permute-start.1 = (bf16[128,896]{1,0:T(8,128)(2,1)S(1)}, bf16[128,896]{1,0:T(8,128)(2,1)S(1)}, u32[]{:S(2)}, u32[]{:S(2)}) collective-permute-start(bf16[128,896]{1,0:T(8,128)(2,1)S(1)} %get-tuple-element.47), channel_id=1, source_target_pairs={{0,7},{1,0},{2,1},{3,2},{4,3},{5,4},{6,5},{7,6},{8,15},{9,8},{10,9... | collective-permute-start | bytes 688136 | tf_op jit(solution)/shard_map/ppermute | solution.py:32
  27.0 5.9 %collective-permute-done.refs_6_ = bf16[128,896]{1,0:T(8,128)(2,1)S(1)} collective-permute-done((bf16[128,896]{1,0:T(8,128)(2,1)S(1)}, bf16[128,896]{1,0:T(8,128)(2,1)S(1)}, u32[]{:S(2)}, u32[]{:S(2)}) %collective-permute-start) | collective-permute-done | bytes 229408 | tf_op jit(solution)/shard_map/ppermute | solution.py:32
  32.9 5.6 %collective-permute-start.4 = (bf16[128,896]{1,0:T(8,128)(2,1)}, bf16[128,896]{1,0:T(8,128)(2,1)S(1)}, u32[]{:S(2)}, u32[]{:S(2)}) collective-permute-start(bf16[128,896]{1,0:T(8,128)(2,1)} %get-tuple-element.49), channel_id=1, source_target_pairs={{0,4},{1,5},{2,6},{3,7},{4,0},{5,1},{6,2},{7,3},{8,12},{9,13},{10,... | collective-permute-start | bytes 688136 | tf_op jit(solution)/shard_map/ppermute | solution.py:32
  38.5 3.8 %collective-permute-start.6 = (bf16[128,896]{1,0:T(8,128)(2,1)}, bf16[128,896]{1,0:T(8,128)(2,1)}, u32[]{:S(2)}, u32[]{:S(2)}) collective-permute-start(bf16[128,896]{1,0:T(8,128)(2,1)} %get-tuple-element.51), channel_id=1, source_target_pairs={{0,3},{1,4},{2,5},{3,6},{4,7},{5,0},{6,1},{7,2},{8,11},{9,12},{10,... | collective-permute-start | bytes 688136 | tf_op jit(solution)/shard_map/ppermute | solution.py:32
  42.3 0.8 collective-permute-start.2
  43.2 1.2 collective-permute-start.3
  45.3 0.3 fusion.1.hot_ref
  45.6 18.0 %collective-permute-done.3 = f32[448]{0:T(512)S(1)} collective-permute-done((f32[448]{0:T(512)S(1)}, f32[448]{0:T(512)S(1)}, u32[]{:S(2)}, u32[]{:S(2)}) %collective-permute-start.3) | collective-permute-done | bytes 1824 | tf_op jit(solution)/shard_map/ppermute | solution.py:283
  63.6 1.3 collective-permute-start.7
  64.9 1.6 collective-permute-start.8
  66.6 3.1 %maximum_select_fusion = bf16[2,448,1024]{2,1,0:T(8,128)(2,1)} fusion(bf16[1,448,1024]{2,1,0:T(8,128)(2,1)S(1)} %bitcast.53, bf16[1,448,1024]{2,1,0:T(8,128)(2,1)} %param.9, pred[]{:T(512)S(6)} %eq.30), kind=kLoop, calls=%fused_computation | loop fusion | flops 2752512 | bytes 3670017 | tf_op jit(solution)/shard_map/jit(_where)/select_n | solution.py:299
  69.7 3.1 %copy.15 = bf16[896,1024]{0,1:T(8,128)(2,1)S(1)} copy(bf16[896,1024]{1,0:T(8,128)(2,1)} %bitcast.50) | data formatting | bytes 3670016 | tf_op jit(solution)/shard_map/jit(_where)/select_n | solution.py:299
  72.8 1.0 collective-permute-done.5.refs_1_
  73.8 9.1 %collective-permute-done.7.refs_3_ = bf16[128,896]{1,0:T(8,128)(2,1)} collective-permute-done((bf16[128,896]{1,0:T(8,128)(2,1)}, bf16[128,896]{1,0:T(8,128)(2,1)}, u32[]{:S(2)}, u32[]{:S(2)}) %collective-permute-start.7) | collective-permute-done | bytes 229408 | tf_op jit(solution)/shard_map/ppermute | solution.py:32
  82.9 3.9 %collective-permute-done.8.refs_4_ = bf16[128,896]{1,0:T(8,128)(2,1)} collective-permute-done((bf16[128,896]{1,0:T(8,128)(2,1)}, bf16[128,896]{1,0:T(8,128)(2,1)}, u32[]{:S(2)}, u32[]{:S(2)}) %collective-permute-start.8) | collective-permute-done | bytes 229408 | tf_op jit(solution)/shard_map/ppermute | solution.py:32
  86.8 2.0 shard_map.88
  88.9 1.6 copy-done.5
  90.5 7.4 %all-to-all-start.1 = ((bf16[8,8,24,896]{3,2,1,0:T(8,128)(2,1)}), bf16[8,8,24,896]{3,2,1,0:T(8,128)(2,1)}, u32[]{:S(2)}, u32[]{:S(2)}) async-start(bf16[8,8,24,896]{3,2,1,0:T(8,128)(2,1)} %copy-done.5), calls=%async_computation.1 | async-start | bytes 5505024 | tf_op jit(solution)/shard_map/all_to_all | solution.py:308
  97.9 31.3 %all-to-all-done.1 = bf16[8,8,24,896]{3,2,1,0:T(8,128)(2,1)} async-done(((bf16[8,8,24,896]{3,2,1,0:T(8,128)(2,1)}), bf16[8,8,24,896]{3,2,1,0:T(8,128)(2,1)}, u32[]{:S(2)}, u32[]{:S(2)}) %all-to-all-start.1) | async-done | bytes 2752544 | tf_op jit(solution)/shard_map/all_to_all | solution.py:308
  129.2 3.7 %copy.16 = bf16[8,8,24,896]{3,2,1,0:T(8,128)(2,1)} copy(bf16[8,8,24,896]{3,2,0,1:T(8,128)(2,1)} %bitcast.12) | data formatting | bytes 5505024 | tf_op jit(solution)/shard_map/transpose | solution.py:309
  132.9 1.1 all-gather.2.cloned.1.call-done
  133.9 2.8 %copy-done.1 = bf16[3072,1024]{1,0:T(8,128)(2,1)S(1)} copy-done((bf16[3072,1024]{1,0:T(8,128)(2,1)S(1)}, bf16[3072,1024]{1,0:T(8,128)(2,1)}, u32[]{:S(2)}) %copy-start.1) | copy-done | bytes 6291480
  136.7 2.7 %shard_map.90 = (f32[576,896]{1,0:T(8,128)S(1)}, s32[3]{0:T(128)S(1)}) custom-call(s32[3]{0:T(128)S(1)} %and_select_fusion.1.place_ref.next_ref, s32[1]{0:T(128)} %bitcast.1.core_ref, s32[3]{0:T(128)S(1)} %and_select_fusion.1.place_ref.next_ref, bf16[1024,896]{1,0:T(8,128)(2,1)S(1)} %bitcast.42, f32[1,896]{1,0:T(1,128)S(1)} %select_n.79.scales_ref, ...), custom_call_target="tpu_custom_call" | custom-call | tf_op jit(solution)/shard_map/pallas_call | solution.py:136
  139.4 0.3 collective-permute-start.11
  139.7 4.0 %collective-permute-done.11.refs_3_ = f32[576,896]{1,0:T(8,128)S(1)} collective-permute-done((f32[576,896]{1,0:T(8,128)S(1)}, f32[576,896]{1,0:T(8,128)S(1)}, u32[]{:S(2)}, u32[]{:S(2)}) %collective-permute-start.11) | collective-permute-done | bytes 2064416 | tf_op jit(solution)/shard_map/ppermute | solution.py:326
  143.8 2.7 %shard_map.91 = (bf16[8,3,24,896]{3,2,1,0:T(8,128)(2,1)S(1)}, s32[5]{0:T(128)S(1)}) custom-call(s32[3]{0:T(128)S(1)} %get-tuple-element.68.place_ref.next_ref, s32[1]{0:T(128)} %bitcast.1.core_ref, s32[5]{0:T(128)S(1)} %and_select_fusion.next_ref, bf16[1024,896]{1,0:T(8,128)(2,1)S(1)} %bitcast.43, f32[1,896]{1,0:T(1,128)S(1)} %select_n.79.scales_ref, ...), custom_call_target="tpu_custom_call" | custom-call | tf_op jit(solution)/shard_map/pallas_call | solution.py:136
  146.5 1.0 copy-done.8
  147.4 5.0 %shard_map.92 = (f32[960,896]{1,0:T(8,128)}, s32[5]{0:T(128)S(1)}) custom-call(s32[5]{0:T(128)S(1)} %get-tuple-element.70.place_ref.next_ref, s32[1]{0:T(128)} %bitcast.1.core_ref, s32[5]{0:T(128)S(1)} %get-tuple-element.70.place_ref.next_ref, bf16[1024,896]{1,0:T(8,128)(2,1)S(1)} %bitcast.44, f32[1,896]{1,0:T(1,128)S(1)} %select_n.79.scales_ref, ...), custom_call_target="tpu_custom_call" | custom-call | tf_op jit(solution)/shard_map/pallas_call | solution.py:136
  152.4 0.2 collective-permute-start.12
  152.7 0.4 collective-permute-start.9
  153.0 6.6 %all-to-all-start.3 = ((bf16[8,3,24,896]{3,2,1,0:T(8,128)(2,1)}), bf16[8,3,24,896]{3,2,1,0:T(8,128)(2,1)S(1)}, u32[]{:S(2)}, u32[]{:S(2)}) async-start(bf16[8,3,24,896]{3,2,1,0:T(8,128)(2,1)} %copy-done.8), calls=%async_computation.3 | async-start | bytes 2064384 | tf_op jit(solution)/shard_map/all_to_all | solution.py:331
  159.7 3.2 %collective-permute-done.9.mate_ref = bf16[1536,896]{1,0:T(8,128)(2,1)} collective-permute-done((bf16[1536,896]{1,0:T(8,128)(2,1)}, bf16[1536,896]{1,0:T(8,128)(2,1)}, u32[]{:S(2)}, u32[]{:S(2)}) %collective-permute-start.9) | collective-permute-done | bytes 2752544 | tf_op jit(solution)/shard_map/ppermute | solution.py:310
  162.9 9.8 %shard_map.89 = f32[896,1024]{1,0:T(8,128)S(1)} custom-call(s32[1]{0:T(128)} %bitcast.1.core_ref, bf16[8,2,192,1024]{3,2,1,0:T(8,128)(2,1)} %bitcast.25, bf16[1536,896]{1,0:T(8,128)(2,1)} %bitcast.13.own_ref, bf16[1536,896]{1,0:T(8,128)(2,1)} %collective-permute-done.9.mate_ref), custom_call_target="tpu_custom_call" | custom-call | tf_op jit(solution)/shard_map/pallas_call | solution.py:168
  172.7 1.9 copy-done.4
  174.6 2.8 %copy-done.3 = bf16[3072,1024]{1,0:T(8,128)(2,1)S(1)} copy-done((bf16[3072,1024]{1,0:T(8,128)(2,1)S(1)}, bf16[3072,1024]{1,0:T(8,128)(2,1)}, u32[]{:S(2)}) %copy-start.3) | copy-done | bytes 6291480
  177.4 4.7 %shard_map.93 = (bf16[8,5,24,896]{3,2,1,0:T(8,128)(2,1)S(1)}, s32[3]{0:T(128)}) custom-call(s32[5]{0:T(128)S(1)} %get-tuple-element.71.place_ref, s32[1]{0:T(128)} %bitcast.1.core_ref, s32[3]{0:T(128)S(1)} %get-tuple-element.68.place_ref.next_ref, bf16[1024,896]{1,0:T(8,128)(2,1)S(1)} %bitcast.45, f32[1,896]{1,0:T(1,128)S(1)} %select_n.79.scales_ref, ...), custom_call_target="tpu_custom_call" | custom-call | tf_op jit(solution)/shard_map/pallas_call | solution.py:136
  182.2 1.2 copy-done.7
  183.4 6.7 %all-to-all-start.2 = ((bf16[8,5,24,896]{3,2,1,0:T(8,128)(2,1)}), bf16[8,5,24,896]{3,2,1,0:T(8,128)(2,1)S(1)}, u32[]{:S(2)}, u32[]{:S(2)}) async-start(bf16[8,5,24,896]{3,2,1,0:T(8,128)(2,1)} %copy-done.7), calls=%async_computation.2 | async-start | bytes 3440640 | tf_op jit(solution)/shard_map/all_to_all | solution.py:333
  190.1 0.3 fusion.2
  190.4 1.0 shard_map.94
  191.4 4.1 %collective-permute-start.13 = (bf16[128,896]{1,0:T(8,128)(2,1)}, bf16[128,896]{1,0:T(8,128)(2,1)S(1)}, u32[]{:S(2)}, u32[]{:S(2)}) collective-permute-start(bf16[128,896]{1,0:T(8,128)(2,1)} %get-tuple-element.77), channel_id=1, source_target_pairs={{0,4},{1,5},{2,6},{3,7},{4,0},{5,1},{6,2},{7,3},{8,12},{9,13},{10,... | collective-permute-start | bytes 688136 | tf_op jit(solution)/shard_map/ppermute | solution.py:32
  195.6 1.3 collective-permute-start.14
  196.9 3.7 %collective-permute-start.15 = (bf16[128,896]{1,0:T(8,128)(2,1)S(1)}, bf16[128,896]{1,0:T(8,128)(2,1)S(1)}, u32[]{:S(2)}, u32[]{:S(2)}) collective-permute-start(bf16[128,896]{1,0:T(8,128)(2,1)S(1)} %get-tuple-element.79), channel_id=1, source_target_pairs={{0,5},{1,6},{2,7},{3,0},{4,1},{5,2},{6,3},{7,4},{8,13},{9,14},{10,... | collective-permute-start | bytes 688136 | tf_op jit(solution)/shard_map/ppermute | solution.py:32
  200.6 2.2 abs_reduce_fusion
  203.5 5.6 %collective-permute-start.10 = (f32[1]{0:T(128)}, f32[1]{0:T(128)}, u32[]{:S(2)}, u32[]{:S(2)}) collective-permute-start(f32[1]{0:T(128)} %bitcast.15), channel_id=1, source_target_pairs={{0,8},{8,0},{1,9},{9,1},{2,10},{10,2},{3,11},{11,3},{4,12},{12,4},... | collective-permute-start | bytes 20 | tf_op jit(solution)/shard_map/ppermute | solution.py:341
  209.1 4.2 %dynamic-slice_bitcast_fusion = (f32[448,1024]{1,0:T(8,128)}, f16[448,1024]{1,0:T(8,128)(2,1)}) fusion(f32[2,448,1024]{2,1,0:T(8,128)} %bitcast.47, s32[]{:T(128)S(6)} %select_n.81, f32[]{:T(128)} %bitcast.16, s32[]{:T(128)S(6)} %select_n.80), kind=kLoop, calls=%fused_computation.2 | loop fusion | flops 917504 | bytes 6422540 | tf_op jit(solution)/shard_map/jit(dynamic_index_in_dim)/squeeze | solution.py:338
  213.4 9.2 %collective-permute-done.14.refs_2_ = bf16[128,896]{1,0:T(8,128)(2,1)S(1)} collective-permute-done((bf16[128,896]{1,0:T(8,128)(2,1)S(1)}, bf16[128,896]{1,0:T(8,128)(2,1)S(1)}, u32[]{:S(2)}, u32[]{:S(2)}) %collective-permute-start.14) | collective-permute-done | bytes 229408 | tf_op jit(solution)/shard_map/ppermute | solution.py:32
  222.6 0.9 collective-permute-start.16
  223.6 0.5 shard_map.95
  224.1 0.8 collective-permute-start.17
  224.9 2.4 collective-permute-start.18
  227.3 3.4 %collective-permute-start.19 = (bf16[128,896]{1,0:T(8,128)(2,1)S(1)}, bf16[128,896]{1,0:T(8,128)(2,1)S(1)}, u32[]{:S(2)}, u32[]{:S(2)}) collective-permute-start(bf16[128,896]{1,0:T(8,128)(2,1)S(1)} %get-tuple-element.87), channel_id=1, source_target_pairs={{0,7},{1,0},{2,1},{3,2},{4,3},{5,4},{6,5},{7,6},{8,15},{9,8},{10,9... | collective-permute-start | bytes 688136 | tf_op jit(solution)/shard_map/ppermute | solution.py:32
  230.7 14.2 %collective-permute-done.16 = f16[448,1024]{1,0:T(8,128)(2,1)S(1)} collective-permute-done((f16[448,1024]{1,0:T(8,128)(2,1)}, f16[448,1024]{1,0:T(8,128)(2,1)S(1)}, u32[]{:S(2)}, u32[]{:S(2)}) %collective-permute-start.16) | collective-permute-done | bytes 917536 | tf_op jit(solution)/shard_map/ppermute | solution.py:343
  244.9 2.1 multiply_add_fusion
  247.1 1.8 shard_map.96
  (68 shorter events, 1.4 us)
Async XLA Ops:
  7.2 0.7 copy-start
  7.2 11.3 %copy-start.6 = (bf16[128,7168]{1,0:T(8,128)(2,1)S(1)}, bf16[128,7168]{1,0:T(8,128)(2,1)}, u32[]{:S(2)}) copy-start(bf16[128,7168]{1,0:T(8,128)(2,1)} %hidden_ref.1) | copy-start | bytes 5505028
  8.1 1.0 copy-start.9
  10.9 32.3 %copy-start.15 = (f32[1,448]{1,0:T(1,128)S(1)}, f32[1,448]{1,0:T(1,128)}, u32[]{:S(2)}) copy-start(f32[1,448]{1,0:T(1,128)} %param.10) | copy-start | bytes 5380
  10.9 22.0 %all-to-all-start = ((bf16[16,24,1024]{2,1,0:T(8,128)(2,1)}), bf16[16,24,1024]{2,1,0:T(8,128)(2,1)}, u32[]{:S(2)}, u32[]{:S(2)}) async-start(bf16[16,24,1024]{2,1,0:T(8,128)(2,1)} %bitcast.2), calls=%async_computation | async-start | bytes 1572864 | tf_op jit(solution)/shard_map/all_to_all | solution.py:287
  18.4 115.5 %all-gather.2.cloned.1.call-start = ((), (), s32[]{:S(2)}) async-start(), calls=%async_computation.4 | async-start | bytes 7077888 | tf_op jit(solution)/shard_map/all_gather | solution.py:295
  19.7 0.7 copy-start.10
  20.4 0.7 copy-start.11
  21.1 11.8 %collective-permute-start = (bf16[128,896]{1,0:T(8,128)(2,1)S(1)}, bf16[128,896]{1,0:T(8,128)(2,1)S(1)}, u32[]{:S(2)}, u32[]{:S(2)}) collective-permute-start(bf16[128,896]{1,0:T(8,128)(2,1)S(1)} %get-tuple-element.46), channel_id=1, source_target_pairs={{0,1},{1,2},{2,3},{3,4},{4,5},{5,6},{6,7},{7,0},{8,9},{9,10},{10,1... | collective-permute-start | bytes 688136 | tf_op jit(solution)/shard_map/ppermute | solution.py:32
  23.0 9.9 %collective-permute-start.1 = (bf16[128,896]{1,0:T(8,128)(2,1)S(1)}, bf16[128,896]{1,0:T(8,128)(2,1)S(1)}, u32[]{:S(2)}, u32[]{:S(2)}) collective-permute-start(bf16[128,896]{1,0:T(8,128)(2,1)S(1)} %get-tuple-element.47), channel_id=1, source_target_pairs={{0,7},{1,0},{2,1},{3,2},{4,3},{5,4},{6,5},{7,6},{8,15},{9,8},{10,9... | collective-permute-start | bytes 688136 | tf_op jit(solution)/shard_map/ppermute | solution.py:32
  32.9 39.9 %collective-permute-start.4 = (bf16[128,896]{1,0:T(8,128)(2,1)}, bf16[128,896]{1,0:T(8,128)(2,1)S(1)}, u32[]{:S(2)}, u32[]{:S(2)}) collective-permute-start(bf16[128,896]{1,0:T(8,128)(2,1)} %get-tuple-element.49), channel_id=1, source_target_pairs={{0,4},{1,5},{2,6},{3,7},{4,0},{5,1},{6,2},{7,3},{8,12},{9,13},{10,... | collective-permute-start | bytes 688136 | tf_op jit(solution)/shard_map/ppermute | solution.py:32
  38.5 35.3 %collective-permute-start.5 = (bf16[128,896]{1,0:T(8,128)(2,1)}, bf16[128,896]{1,0:T(8,128)(2,1)S(1)}, u32[]{:S(2)}, u32[]{:S(2)}) collective-permute-start(bf16[128,896]{1,0:T(8,128)(2,1)} %get-tuple-element.50), channel_id=1, source_target_pairs={{0,5},{1,6},{2,7},{3,0},{4,1},{5,2},{6,3},{7,4},{8,13},{9,14},{10,... | collective-permute-start | bytes 688136 | tf_op jit(solution)/shard_map/ppermute | solution.py:32
  38.5 35.3 %collective-permute-start.6 = (bf16[128,896]{1,0:T(8,128)(2,1)}, bf16[128,896]{1,0:T(8,128)(2,1)}, u32[]{:S(2)}, u32[]{:S(2)}) collective-permute-start(bf16[128,896]{1,0:T(8,128)(2,1)} %get-tuple-element.51), channel_id=1, source_target_pairs={{0,3},{1,4},{2,5},{3,6},{4,7},{5,0},{6,1},{7,2},{8,11},{9,12},{10,... | collective-permute-start | bytes 688136 | tf_op jit(solution)/shard_map/ppermute | solution.py:32
  42.3 22.6 %collective-permute-start.2 = (bf16[448,1024]{1,0:T(8,128)(2,1)}, bf16[448,1024]{1,0:T(8,128)(2,1)S(1)}, u32[]{:S(2)}, u32[]{:S(2)}) collective-permute-start(bf16[448,1024]{1,0:T(8,128)(2,1)} %bitcast.52), channel_id=1, source_target_pairs={{0,8},{8,0},{1,9},{9,1},{2,10},{10,2},{3,11},{11,3},{4,12},{12,4},... | collective-permute-start | bytes 2752520 | tf_op jit(solution)/shard_map/ppermute | solution.py:283
  43.2 20.4 %collective-permute-start.3 = (f32[448]{0:T(512)S(1)}, f32[448]{0:T(512)S(1)}, u32[]{:S(2)}, u32[]{:S(2)}) collective-permute-start(f32[448]{0:T(512)S(1)} %bitcast.54), channel_id=1, source_target_pairs={{0,8},{8,0},{1,9},{9,1},{2,10},{10,2},{3,11},{11,3},{4,12},{12,4},... | collective-permute-start | bytes 5384 | tf_op jit(solution)/shard_map/ppermute | solution.py:283
  63.6 19.3 %collective-permute-start.7 = (bf16[128,896]{1,0:T(8,128)(2,1)}, bf16[128,896]{1,0:T(8,128)(2,1)}, u32[]{:S(2)}, u32[]{:S(2)}) collective-permute-start(bf16[128,896]{1,0:T(8,128)(2,1)} %copy-done.11), channel_id=1, source_target_pairs={{0,6},{1,7},{2,0},{3,1},{4,2},{5,3},{6,4},{7,5},{8,14},{9,15},{10,... | collective-permute-start | bytes 688136 | tf_op jit(solution)/shard_map/ppermute | solution.py:32
  64.9 21.9 %collective-permute-start.8 = (bf16[128,896]{1,0:T(8,128)(2,1)}, bf16[128,896]{1,0:T(8,128)(2,1)}, u32[]{:S(2)}, u32[]{:S(2)}) collective-permute-start(bf16[128,896]{1,0:T(8,128)(2,1)} %copy-done.10), channel_id=1, source_target_pairs={{0,2},{1,3},{2,4},{3,5},{4,6},{5,7},{6,0},{7,1},{8,10},{9,11},{10,... | collective-permute-start | bytes 688136 | tf_op jit(solution)/shard_map/ppermute | solution.py:32
  88.9 1.6 copy-start.5
  90.5 7.4 %copy-start.17 = (s32[3]{0:T(128)S(1)}, s32[3]{0:T(128)}, u32[]{:S(2)}) copy-start(s32[3]{0:T(128)} %constant.80.clone) | copy-start | bytes 40
  90.5 38.7 %all-to-all-start.1 = ((bf16[8,8,24,896]{3,2,1,0:T(8,128)(2,1)}), bf16[8,8,24,896]{3,2,1,0:T(8,128)(2,1)}, u32[]{:S(2)}, u32[]{:S(2)}) async-start(bf16[8,8,24,896]{3,2,1,0:T(8,128)(2,1)} %copy-done.5), calls=%async_computation.1 | async-start | bytes 5505024 | tf_op jit(solution)/shard_map/all_to_all | solution.py:308
  133.9 2.8 %copy-start.1 = (bf16[3072,1024]{1,0:T(8,128)(2,1)S(1)}, bf16[3072,1024]{1,0:T(8,128)(2,1)}, u32[]{:S(2)}) copy-start(bf16[3072,1024]{1,0:T(8,128)(2,1)} %all-gather.2.cloned.1.call-done) | copy-start | bytes 18874372
  136.7 3.0 %copy-start.16 = (s32[5]{0:T(128)S(1)}, s32[5]{0:T(128)}, u32[]{:S(2)}) copy-start(s32[5]{0:T(128)} %constant.81.clone) | copy-start | bytes 64
  136.7 7.1 %copy-start.2 = (bf16[3072,1024]{1,0:T(8,128)(2,1)S(1)}, bf16[3072,1024]{1,0:T(8,128)(2,1)}, u32[]{:S(2)}) copy-start(bf16[3072,1024]{1,0:T(8,128)(2,1)} %all-gather.2.cloned.1.call-done) | copy-start | bytes 18874372
  139.4 4.4 %collective-permute-start.11 = (f32[576,896]{1,0:T(8,128)S(1)}, f32[576,896]{1,0:T(8,128)S(1)}, u32[]{:S(2)}, u32[]{:S(2)}) collective-permute-start(f32[576,896]{1,0:T(8,128)S(1)} %get-tuple-element.69), channel_id=1, source_target_pairs={{0,16},{16,0},{1,17},{17,1},{2,18},{18,2},{3,19},{19,3},{4,20},{20... | collective-permute-start | bytes 6193160 | tf_op jit(solution)/shard_map/ppermute | solution.py:326
  146.5 1.0 copy-start.8
  152.4 22.2 %collective-permute-start.12 = (f32[960,896]{1,0:T(8,128)}, f32[960,896]{1,0:T(8,128)}, u32[]{:S(2)}, u32[]{:S(2)}) collective-permute-start(f32[960,896]{1,0:T(8,128)} %get-tuple-element.72), channel_id=1, source_target_pairs={{0,16},{16,0},{1,17},{17,1},{2,18},{18,2},{3,19},{19,3},{4,20},{20... | collective-permute-start | bytes 10321928 | tf_op jit(solution)/shard_map/ppermute | solution.py:328
  152.7 10.2 %collective-permute-start.9 = (bf16[1536,896]{1,0:T(8,128)(2,1)}, bf16[1536,896]{1,0:T(8,128)(2,1)}, u32[]{:S(2)}, u32[]{:S(2)}) collective-permute-start(bf16[1536,896]{1,0:T(8,128)(2,1)} %bitcast.13.own_ref), channel_id=1, source_target_pairs={{0,16},{16,0},{1,17},{17,1},{2,18},{18,2},{3,19},{19,3},{4,20},{20... | collective-permute-start | bytes 8257544 | tf_op jit(solution)/shard_map/ppermute | solution.py:310
  153.0 30.3 %all-to-all-start.3 = ((bf16[8,3,24,896]{3,2,1,0:T(8,128)(2,1)}), bf16[8,3,24,896]{3,2,1,0:T(8,128)(2,1)S(1)}, u32[]{:S(2)}, u32[]{:S(2)}) async-start(bf16[8,3,24,896]{3,2,1,0:T(8,128)(2,1)} %copy-done.8), calls=%async_computation.3 | async-start | bytes 2064384 | tf_op jit(solution)/shard_map/all_to_all | solution.py:331
  172.7 1.9 copy-start.4
  174.6 2.8 %copy-start.3 = (bf16[3072,1024]{1,0:T(8,128)(2,1)S(1)}, bf16[3072,1024]{1,0:T(8,128)(2,1)}, u32[]{:S(2)}) copy-start(bf16[3072,1024]{1,0:T(8,128)(2,1)} %all-gather.2.cloned.1.call-done) | copy-start | bytes 18874372
  182.2 1.2 copy-start.7
  183.4 39.2 %all-to-all-start.2 = ((bf16[8,5,24,896]{3,2,1,0:T(8,128)(2,1)}), bf16[8,5,24,896]{3,2,1,0:T(8,128)(2,1)S(1)}, u32[]{:S(2)}, u32[]{:S(2)}) async-start(bf16[8,5,24,896]{3,2,1,0:T(8,128)(2,1)} %copy-done.7), calls=%async_computation.2 | async-start | bytes 3440640 | tf_op jit(solution)/shard_map/all_to_all | solution.py:333
  190.4 6.5 %copy-start.13 = (bf16[8,8,24,128]{3,2,1,0:T(8,128)(2,1)}, bf16[8,8,24,128]{3,2,1,0:T(8,128)(2,1)S(1)}, u32[]{:S(2)}) copy-start(bf16[8,8,24,128]{3,2,1,0:T(8,128)(2,1)S(1)} %fusion.2) | copy-start | bytes 1179652
  191.4 21.9 %collective-permute-start.13 = (bf16[128,896]{1,0:T(8,128)(2,1)}, bf16[128,896]{1,0:T(8,128)(2,1)S(1)}, u32[]{:S(2)}, u32[]{:S(2)}) collective-permute-start(bf16[128,896]{1,0:T(8,128)(2,1)} %get-tuple-element.77), channel_id=1, source_target_pairs={{0,4},{1,5},{2,6},{3,7},{4,0},{5,1},{6,2},{7,3},{8,12},{9,13},{10,... | collective-permute-start | bytes 688136 | tf_op jit(solution)/shard_map/ppermute | solution.py:32
  195.6 27.0 %collective-permute-start.14 = (bf16[128,896]{1,0:T(8,128)(2,1)S(1)}, bf16[128,896]{1,0:T(8,128)(2,1)S(1)}, u32[]{:S(2)}, u32[]{:S(2)}) collective-permute-start(bf16[128,896]{1,0:T(8,128)(2,1)S(1)} %get-tuple-element.78), channel_id=1, source_target_pairs={{0,3},{1,4},{2,5},{3,6},{4,7},{5,0},{6,1},{7,2},{8,11},{9,12},{10,... | collective-permute-start | bytes 688136 | tf_op jit(solution)/shard_map/ppermute | solution.py:32
  196.9 25.7 %collective-permute-start.15 = (bf16[128,896]{1,0:T(8,128)(2,1)S(1)}, bf16[128,896]{1,0:T(8,128)(2,1)S(1)}, u32[]{:S(2)}, u32[]{:S(2)}) collective-permute-start(bf16[128,896]{1,0:T(8,128)(2,1)S(1)} %get-tuple-element.79), channel_id=1, source_target_pairs={{0,5},{1,6},{2,7},{3,0},{4,1},{5,2},{6,3},{7,4},{8,13},{9,14},{10,... | collective-permute-start | bytes 688136 | tf_op jit(solution)/shard_map/ppermute | solution.py:32
  203.5 19.1 %collective-permute-start.10 = (f32[1]{0:T(128)}, f32[1]{0:T(128)}, u32[]{:S(2)}, u32[]{:S(2)}) collective-permute-start(f32[1]{0:T(128)} %bitcast.15), channel_id=1, source_target_pairs={{0,8},{8,0},{1,9},{9,1},{2,10},{10,2},{3,11},{11,3},{4,12},{12,4},... | collective-permute-start | bytes 20 | tf_op jit(solution)/shard_map/ppermute | solution.py:341
  209.1 14.4 %copy-start.14 = (bf16[8,8,24,128]{3,2,1,0:T(8,128)(2,1)S(1)}, bf16[8,8,24,128]{3,2,1,0:T(8,128)(2,1)}, u32[]{:S(2)}) copy-start(bf16[8,8,24,128]{3,2,1,0:T(8,128)(2,1)} %copy-done.13) | copy-start | bytes 1179652
  222.6 22.3 %copy-start.12 = (f32[448,1024]{1,0:T(8,128)S(1)}, f32[448,1024]{1,0:T(8,128)}, u32[]{:S(2)}) copy-start(f32[448,1024]{1,0:T(8,128)} %get-tuple-element.81) | copy-start | bytes 5505028
  222.6 22.3 %collective-permute-start.16 = (f16[448,1024]{1,0:T(8,128)(2,1)}, f16[448,1024]{1,0:T(8,128)(2,1)S(1)}, u32[]{:S(2)}, u32[]{:S(2)}) collective-permute-start(f16[448,1024]{1,0:T(8,128)(2,1)} %get-tuple-element.82), channel_id=1, source_target_pairs={{0,8},{8,0},{1,9},{9,1},{2,10},{10,2},{3,11},{11,3},{4,12},{12,4},... | collective-permute-start | bytes 2752520 | tf_op jit(solution)/shard_map/ppermute | solution.py:343
  224.1 23.0 %collective-permute-start.17 = (bf16[128,896]{1,0:T(8,128)(2,1)S(1)}, bf16[128,896]{1,0:T(8,128)(2,1)S(1)}, u32[]{:S(2)}, u32[]{:S(2)}) collective-permute-start(bf16[128,896]{1,0:T(8,128)(2,1)S(1)} %get-tuple-element.85), channel_id=1, source_target_pairs={{0,6},{1,7},{2,0},{3,1},{4,2},{5,3},{6,4},{7,5},{8,14},{9,15},{10,... | collective-permute-start | bytes 688136 | tf_op jit(solution)/shard_map/ppermute | solution.py:32
  224.9 22.2 %collective-permute-start.18 = (bf16[128,896]{1,0:T(8,128)(2,1)S(1)}, bf16[128,896]{1,0:T(8,128)(2,1)S(1)}, u32[]{:S(2)}, u32[]{:S(2)}) collective-permute-start(bf16[128,896]{1,0:T(8,128)(2,1)S(1)} %get-tuple-element.86), channel_id=1, source_target_pairs={{0,2},{1,3},{2,4},{3,5},{4,6},{5,7},{6,0},{7,1},{8,10},{9,11},{10,... | collective-permute-start | bytes 688136 | tf_op jit(solution)/shard_map/ppermute | solution.py:32
  227.3 19.7 %collective-permute-start.19 = (bf16[128,896]{1,0:T(8,128)(2,1)S(1)}, bf16[128,896]{1,0:T(8,128)(2,1)S(1)}, u32[]{:S(2)}, u32[]{:S(2)}) collective-permute-start(bf16[128,896]{1,0:T(8,128)(2,1)S(1)} %get-tuple-element.87), channel_id=1, source_target_pairs={{0,7},{1,0},{2,1},{3,2},{4,3},{5,4},{6,5},{7,6},{8,15},{9,8},{10,9... | collective-permute-start | bytes 688136 | tf_op jit(solution)/shard_map/ppermute | solution.py:32
  230.7 16.4 %collective-permute-start.20 = (bf16[128,896]{1,0:T(8,128)(2,1)S(1)}, bf16[128,896]{1,0:T(8,128)(2,1)S(1)}, u32[]{:S(2)}, u32[]{:S(2)}) collective-permute-start(bf16[128,896]{1,0:T(8,128)(2,1)S(1)} %get-tuple-element.88), channel_id=1, source_target_pairs={{0,1},{1,2},{2,3},{3,4},{4,5},{5,6},{6,7},{7,0},{8,9},{9,10},{10,1... | collective-permute-start | bytes 688136 | tf_op jit(solution)/shard_map/ppermute | solution.py:32
Sparse Core Ops, SparseCore 0:
  33.0 100.8 all-gather.1
where the time goes:
time: 256 us
  waiting for transfers between devices  101 us (39%)
  starting transfers between devices  71.7 us (28%)
  Pallas kernels  33.3 us (13%)
  local copies, waits for them, and re-layouts  22.2 us (9%)
  between operations  15 us (6%)
  other arithmetic  12.5 us (5%)
    ppermute x14, starting transfers between devices, along_z(): lax.ppermute(value, 'z', [(i, (i + by) % depth) for i in range(depth)])  33.9 us
    all_to_all x1, waiting for transfers between devices, shards(): own_hidden = lax.all_to_all(hidden_slots, PLACES, 0, 0)  31.3 us
    ppermute x14, waiting for transfers between devices, along_z(): lax.ppermute(value, 'z', [(i, (i + by) % depth) for i in range(depth)])  29.2 us
    ppermute x2, waiting for transfers between devices, shards(): other_codes, other_scales = lax.ppermute((codes[0], scales[0]), 'xl', SWAP)  18 us
    pallas_call x4, Pallas kernels, partials(): pl.pallas_call(kernel, out_shape=[jax.ShapeDtypeStruct(shape, dtype), jax...  15.1 us
    unnamed x36, local copies, waits for them, and re-layouts  14.3 us
    ppermute x1, waiting for transfers between devices, shards(): gone = lax.ppermute(gone, 'xl', SWAP)  14.2 us
    pallas_call x1, Pallas kernels, weight_sums(): pl.pallas_call(weight_kernel, out_shape=jax.ShapeDtypeStruct((wide, half)...  9.85 us
  transfers between devices with their start and end apart: 26, of which 11 were waited for; matrix products, arithmetic and copies ran while one was open for 8% of the time, Pallas kernels for 8%

commit v1 on v0

--- a/solution.py
+++ b/solution.py
@@ -129,13 +129,14 @@
     in_specs = [words, whole(half, wide), whole(1, wide)] + [rows_spec(j) for j in range(steps)]
     if mate is None:
         kernel, shape, dtype, extra = mate_kernel, (steps * rows, wide), jnp.float32, ()
+        place = jax.ShapeDtypeStruct
     else:
-        kernel, extra = own_kernel, (mate,)
+        kernel, extra, place = own_kernel, (mate,), pltpu.HBM
         in_specs.append(whole(steps * rows, wide))
         shape, dtype = (places, steps, rows // places, wide), jnp.bfloat16
     return pl.pallas_call(
         kernel,
-        out_shape=[jax.ShapeDtypeStruct(shape, dtype), jax.ShapeDtypeStruct(then.shape, then.dtype)],
+        out_shape=[place(shape, dtype), jax.ShapeDtypeStruct(then.shape, then.dtype)],
         grid_spec=pltpu.PrefetchScalarGridSpec(
             num_scalar_prefetch=2, grid=(1,), in_specs=in_specs, out_specs=[whole(*shape), words]
         ),
@@ -167,7 +168,7 @@
     units = pl.BlockSpec((levels * rows, wide), lambda i, c: (i, 0))
     return pl.pallas_call(
         weight_kernel,
-        out_shape=jax.ShapeDtypeStruct((wide, half), jnp.float32),
+        out_shape=pltpu.HBM((wide, half), jnp.float32),
         grid_spec=pltpu.PrefetchScalarGridSpec(
             num_scalar_prefetch=1,
             grid=(depth // levels,),
@@ -248,7 +249,7 @@
     whole = pl.BlockSpec(memory_space=pltpu.VMEM)
     return pl.pallas_call(
         pack_kernel,
-        out_shape=jax.ShapeDtypeStruct((experts, depth, places // experts, wide), jnp.bfloat16),
+        out_shape=pltpu.HBM((experts, depth, places // experts, wide), jnp.bfloat16),
         in_specs=[pl.BlockSpec(memory_space=pltpu.SMEM)] + [whole] * (depth + 1),
         out_specs=whole,
         compiler_params=pltpu.CompilerParams(vmem_limit_bytes=40 << 20),
@@ -310,7 +311,9 @@
     mate_hidden = lax.ppermute(own_hidden, "c", SWAP)
     values = after(values, own_hidden)
 
-    def product(where, then, *mate):
+    pinned = pltpu.with_memory_space_constraint(values, pltpu.HBM)
+
+    def product(values, where, then, *mate):
         args = (where, core_word, then, values, both_codes, both_scales)
         return partials(*args, *mate, places) if mate else partials(*args)
 
@@ -322,18 +325,18 @@
 
     cut = 3
     far_at, close_at = levels_at(order[:cut]), levels_at(order[cut:])
-    far_mate, far_at = product(far_at, far_at)
-    far_joined, close_at = product(far_at, close_at, lax.ppermute(far_mate, "c", SWAP))
-    close_mate, close_at = product(close_at, close_at)
-    close_joined, _ = product(close_at, far_at, lax.ppermute(close_mate, "c", SWAP))
-    sums = weight_sums(core_word, values, own_hidden, mate_hidden)
-    close_joined = after(close_joined, sums)
-    far_raw = after(lax.all_to_all(far_joined, PLACES, 0, 0), close_joined, sums)
-    send_home(order[:cut], unpack(near_hot[:cut], far_raw))
+    far_mate, far_at = product(pinned, far_at, far_at)
+    far_joined, close_at = product(values, far_at, close_at, lax.ppermute(far_mate, "c", SWAP))
+    close_mate, close_at = product(values, close_at, close_at)
+    close_joined, _ = product(pinned, close_at, far_at, lax.ppermute(close_mate, "c", SWAP))
+    far_raw = after(lax.all_to_all(far_joined, PLACES, 0, 0), close_joined)
+    far_back = unpack(near_hot[:cut], far_raw)
+    send_home(order[:cut], far_back)
     close_raw = after(lax.all_to_all(close_joined, PLACES, 0, 0), *came.values())
     send_home(order[cut:], unpack(near_hot[cut:], close_raw))
 
-    sums = sums.reshape(2, share, half)
+    own_hidden, mate_hidden = after((own_hidden, mate_hidden), *far_back)
+    sums = weight_sums(core_word, pinned, own_hidden, mate_hidden).reshape(2, share, half)
     gone = lax.dynamic_index_in_dim(sums, 1 - side, 0, keepdims=False)
     kept = lax.dynamic_index_in_dim(sums, side, 0, keepdims=False)
     largest = jnp.maximum(jnp.max(jnp.abs(gone)), 1e-30).reshape(1)

time: 256 us -> 244 us (0.953)
  local copies, waits for them, and re-layouts: 22.2 us -> 10.9 us
  Pallas kernels: 33.3 us -> 40.2 us
  starting transfers between devices: 71.7 us -> 67.2 us
  waiting for transfers between devices: 101 us -> 97.7 us
    unnamed x36 -> x26, local copies, waits for them, and re-layouts: 14.3 us -> 3.11 us
    ppermute x14, waiting for transfers between devices: 29.2 us -> 20.9 us  [along_z(): lax.ppermute(value, 'z', [(i, (i + by) % depth) for i in range(depth)])]
    all_to_all x1, waiting for transfers between devices: 0.01 us -> 8.1 us  [shards(): far_raw = after(lax.all_to_all(far_joined, PLACES, 0, 0), close_joined)]
    pallas_call x6, Pallas kernels: 27 us -> 33.9 us  [the longest x4 18.9 us: partials(): pl.pallas_call(kernel, out_shape=[place(shape, dtype), jax.ShapeDtypeStru...]
    ppermute x1, starting transfers between devices: 5.58 us -> 2.19 us  [shards(): largest = lax.ppermute(largest, 'xl', SWAP)]
    ppermute x1, waiting for transfers between devices: 3.22 us -> 0.01 us  [shards(): mate_hidden = lax.ppermute(own_hidden, 'c', SWAP)]
  transfers between devices with their start and end apart: 26 -> 26, of which waited for: 11 -> 11; matrix products, arithmetic and copies ran while one was open for 8% -> 8% of each run, Pallas kernels for 8% -> 10%
where the time goes in v1:
time: 244 us; the launch traced here: 243 us
  waiting for transfers between devices  97.7 us (40%)
  starting transfers between devices  67.2 us (28%)
  Pallas kernels  40.2 us (16%)
  between operations  15 us (6%)
  other arithmetic  12.5 us (5%)
  local copies, waits for them, and re-layouts  10.9 us (4%)
    ppermute x14, starting transfers between devices, along_z(): lax.ppermute(value, 'z', [(i, (i + by) % depth) for i in range(depth)])  33.9 us
    all_to_all x1, waiting for transfers between devices, shards(): own_hidden = lax.all_to_all(hidden_slots, PLACES, 0, 0)  31.3 us
    ppermute x14, waiting for transfers between devices, along_z(): lax.ppermute(value, 'z', [(i, (i + by) % depth) for i in range(depth)])  20.9 us
    pallas_call x4, Pallas kernels, partials(): pl.pallas_call(kernel, out_shape=[place(shape, dtype), jax.ShapeDtypeStru...  18.9 us
    ppermute x2, waiting for transfers between devices, shards(): other_codes, other_scales = lax.ppermute((codes[0], scales[0]), 'xl', SWAP)  18 us
    ppermute x1, waiting for transfers between devices, shards(): gone = lax.ppermute(gone, 'xl', SWAP)  14.1 us
    pallas_call x1, Pallas kernels, weight_sums(): pl.pallas_call(weight_kernel, out_shape=pltpu.HBM((wide, half), jnp.float...  11.5 us
    all_to_all x1, waiting for transfers between devices, shards(): far_raw = after(lax.all_to_all(far_joined, PLACES, 0, 0), close_joined)  8.1 us
  transfers between devices with their start and end apart: 26, of which 11 were waited for; matrix products, arithmetic and copies ran while one was open for 8% of the time, Pallas kernels for 10%

profile of v1, /device:TPU:6, one launch (start us, length us, event | category | flops | bytes accessed | tf_op | source)
XLA Modules:
  0.0 243.5 jit_solution(10033403039429753782)
XLA Ops:
  7.2 0.7 copy-done
  7.9 0.2 dynamic-slice_reduce_fusion.counts_ref
  8.1 1.0 copy-done.2
  9.1 1.8 shard_map.86
  10.9 7.6 %all-to-all-start = ((bf16[16,24,1024]{2,1,0:T(8,128)(2,1)}), bf16[16,24,1024]{2,1,0:T(8,128)(2,1)}, u32[]{:S(2)}, u32[]{:S(2)}) async-start(bf16[16,24,1024]{2,1,0:T(8,128)(2,1)} %bitcast.2), calls=%async_computation | async-start | bytes 1572864 | tf_op jit(solution)/shard_map/all_to_all | solution.py:288
  18.5 1.2 shard_map.87
  19.7 0.7 copy-done.3
  20.4 0.7 copy-done.4
  21.1 1.9 collective-permute-start
  23.0 3.9 %collective-permute-start.1 = (bf16[128,896]{1,0:T(8,128)(2,1)S(1)}, bf16[128,896]{1,0:T(8,128)(2,1)S(1)}, u32[]{:S(2)}, u32[]{:S(2)}) collective-permute-start(bf16[128,896]{1,0:T(8,128)(2,1)S(1)} %get-tuple-element.48), channel_id=1, source_target_pairs={{0,7},{1,0},{2,1},{3,2},{4,3},{5,4},{6,5},{7,6},{8,15},{9,8},{10,9... | collective-permute-start | bytes 688136 | tf_op jit(solution)/shard_map/ppermute | solution.py:32
  27.0 5.9 %collective-permute-done.refs_6_ = bf16[128,896]{1,0:T(8,128)(2,1)S(1)} collective-permute-done((bf16[128,896]{1,0:T(8,128)(2,1)S(1)}, bf16[128,896]{1,0:T(8,128)(2,1)S(1)}, u32[]{:S(2)}, u32[]{:S(2)}) %collective-permute-start) | collective-permute-done | bytes 229408 | tf_op jit(solution)/shard_map/ppermute | solution.py:32
  32.9 5.6 %collective-permute-start.4 = (bf16[128,896]{1,0:T(8,128)(2,1)}, bf16[128,896]{1,0:T(8,128)(2,1)S(1)}, u32[]{:S(2)}, u32[]{:S(2)}) collective-permute-start(bf16[128,896]{1,0:T(8,128)(2,1)} %get-tuple-element.50), channel_id=1, source_target_pairs={{0,4},{1,5},{2,6},{3,7},{4,0},{5,1},{6,2},{7,3},{8,12},{9,13},{10,... | collective-permute-start | bytes 688136 | tf_op jit(solution)/shard_map/ppermute | solution.py:32
  38.5 3.8 %collective-permute-start.6 = (bf16[128,896]{1,0:T(8,128)(2,1)}, bf16[128,896]{1,0:T(8,128)(2,1)}, u32[]{:S(2)}, u32[]{:S(2)}) collective-permute-start(bf16[128,896]{1,0:T(8,128)(2,1)} %get-tuple-element.52), channel_id=1, source_target_pairs={{0,3},{1,4},{2,5},{3,6},{4,7},{5,0},{6,1},{7,2},{8,11},{9,12},{10,... | collective-permute-start | bytes 688136 | tf_op jit(solution)/shard_map/ppermute | solution.py:32
  42.3 0.8 collective-permute-start.2
  43.2 1.2 collective-permute-start.3
  44.4 0.1 pad_add_fusion
  44.7 0.1 stack.23
  45.1 0.1 lt.70
  45.2 0.1 lt.66
  45.3 0.3 fusion.1.hot_ref
  45.6 18.0 %collective-permute-done.3 = f32[448]{0:T(512)S(1)} collective-permute-done((f32[448]{0:T(512)S(1)}, f32[448]{0:T(512)S(1)}, u32[]{:S(2)}, u32[]{:S(2)}) %collective-permute-start.3) | collective-permute-done | bytes 1824 | tf_op jit(solution)/shard_map/ppermute | solution.py:284
  63.6 1.3 collective-permute-start.7
  64.9 1.6 collective-permute-start.8
  66.5 0.1 select_n.79.scales_ref
  66.6 3.1 %maximum_select_fusion = bf16[2,448,1024]{2,1,0:T(8,128)(2,1)} fusion(bf16[1,448,1024]{2,1,0:T(8,128)(2,1)S(1)} %bitcast.55, bf16[1,448,1024]{2,1,0:T(8,128)(2,1)} %param.9, pred[]{:T(512)S(6)} %eq.30), kind=kLoop, calls=%fused_computation | loop fusion | flops 2752512 | bytes 3670017 | tf_op jit(solution)/shard_map/jit(_where)/select_n | solution.py:300
  69.7 3.1 %copy.15 = bf16[896,1024]{0,1:T(8,128)(2,1)S(1)} copy(bf16[896,1024]{1,0:T(8,128)(2,1)} %bitcast.52) | data formatting | bytes 3670016 | tf_op jit(solution)/shard_map/jit(_where)/select_n | solution.py:300
  72.7 1.0 collective-permute-done.5.refs_1_
  73.8 9.1 %collective-permute-done.7.refs_3_ = bf16[128,896]{1,0:T(8,128)(2,1)} collective-permute-done((bf16[128,896]{1,0:T(8,128)(2,1)}, bf16[128,896]{1,0:T(8,128)(2,1)}, u32[]{:S(2)}, u32[]{:S(2)}) %collective-permute-start.7) | collective-permute-done | bytes 229408 | tf_op jit(solution)/shard_map/ppermute | solution.py:32
  82.9 3.9 %collective-permute-done.8.refs_4_ = bf16[128,896]{1,0:T(8,128)(2,1)} collective-permute-done((bf16[128,896]{1,0:T(8,128)(2,1)}, bf16[128,896]{1,0:T(8,128)(2,1)}, u32[]{:S(2)}, u32[]{:S(2)}) %collective-permute-start.8) | collective-permute-done | bytes 229408 | tf_op jit(solution)/shard_map/ppermute | solution.py:32
  86.8 3.6 %shard_map.88 = bf16[8,8,24,896]{3,2,1,0:T(8,128)(2,1)} custom-call(s32[1]{0:T(128)} %bitcast.level_ref, bf16[8,192,128]{2,1,0:T(8,128)(2,1)S(1)} %fusion.1.hot_ref, bf16[128,896]{1,0:T(8,128)(2,1)S(1)} %collective-permute-done.4.refs_0_, bf16[128,896]{1,0:T(8,128)(2,1)S(1)} %collective-permute-done.5.refs_1_, ...), custom_call_target="tpu_custom_call" | custom-call | tf_op jit(solution)/shard_map/pallas_call | solution.py:250
  90.4 7.4 %all-to-all-start.1 = ((bf16[8,8,24,896]{3,2,1,0:T(8,128)(2,1)}), bf16[8,8,24,896]{3,2,1,0:T(8,128)(2,1)}, u32[]{:S(2)}, u32[]{:S(2)}) async-start(bf16[8,8,24,896]{3,2,1,0:T(8,128)(2,1)} %shard_map.88), calls=%async_computation.1 | async-start | bytes 5505024 | tf_op jit(solution)/shard_map/all_to_all | solution.py:309
  97.9 31.3 %all-to-all-done.1 = bf16[8,8,24,896]{3,2,1,0:T(8,128)(2,1)} async-done(((bf16[8,8,24,896]{3,2,1,0:T(8,128)(2,1)}), bf16[8,8,24,896]{3,2,1,0:T(8,128)(2,1)}, u32[]{:S(2)}, u32[]{:S(2)}) %all-to-all-start.1) | async-done | bytes 2752544 | tf_op jit(solution)/shard_map/all_to_all | solution.py:309
  129.2 3.6 %copy.16 = bf16[8,8,24,896]{3,2,1,0:T(8,128)(2,1)} copy(bf16[8,8,24,896]{3,2,0,1:T(8,128)(2,1)} %bitcast.12) | data formatting | bytes 5505024 | tf_op jit(solution)/shard_map/transpose | solution.py:310
  132.7 1.2 all-gather.2.cloned.1.call-done
  133.9 3.7 %shard_map.89 = (f32[576,896]{1,0:T(8,128)S(1)}, s32[3]{0:T(128)S(1)}) custom-call(s32[3]{0:T(128)S(1)} %and_select_fusion.1.place_ref.next_ref, s32[1]{0:T(128)} %bitcast.1.core_ref, s32[3]{0:T(128)S(1)} %and_select_fusion.1.place_ref.next_ref, bf16[1024,896]{1,0:T(8,128)(2,1)S(1)} %bitcast.44, f32[1,896]{1,0:T(1,128)S(1)} %select_n.79.scales_ref, ...), custom_call_target="tpu_custom_call" | custom-call | tf_op jit(solution)/shard_map/pallas_call | solution.py:137
  137.6 0.3 collective-permute-start.10
  137.9 4.0 %collective-permute-done.10.refs_3_ = f32[576,896]{1,0:T(8,128)S(1)} collective-permute-done((f32[576,896]{1,0:T(8,128)S(1)}, f32[576,896]{1,0:T(8,128)S(1)}, u32[]{:S(2)}, u32[]{:S(2)}) %collective-permute-start.10) | collective-permute-done | bytes 2064416 | tf_op jit(solution)/shard_map/ppermute | solution.py:329
  142.0 3.5 %shard_map.90 = (bf16[8,3,24,896]{3,2,1,0:T(8,128)(2,1)}, s32[5]{0:T(128)S(1)}) custom-call(s32[3]{0:T(128)S(1)} %get-tuple-element.69.place_ref.next_ref, s32[1]{0:T(128)} %bitcast.1.core_ref, s32[5]{0:T(128)S(1)} %and_select_fusion.next_ref, bf16[1024,896]{1,0:T(8,128)(2,1)S(1)} %bitcast.45, f32[1,896]{1,0:T(1,128)S(1)} %select_n.79.scales_ref, ...), custom_call_target="tpu_custom_call" | custom-call | tf_op jit(solution)/shard_map/pallas_call | solution.py:137
  145.5 5.2 %shard_map.91 = (f32[960,896]{1,0:T(8,128)}, s32[5]{0:T(128)S(1)}) custom-call(s32[5]{0:T(128)S(1)} %get-tuple-element.72.place_ref.next_ref, s32[1]{0:T(128)} %bitcast.1.core_ref, s32[5]{0:T(128)S(1)} %get-tuple-element.72.place_ref.next_ref, bf16[1024,896]{1,0:T(8,128)(2,1)S(1)} %bitcast.46, f32[1,896]{1,0:T(1,128)S(1)} %select_n.79.scales_ref, ...), custom_call_target="tpu_custom_call" | custom-call | tf_op jit(solution)/shard_map/pallas_call | solution.py:137
  150.6 0.2 collective-permute-start.11
  150.9 0.4 collective-permute-start.9
  151.2 6.6 %all-to-all-start.2 = ((bf16[8,3,24,896]{3,2,1,0:T(8,128)(2,1)}), bf16[8,3,24,896]{3,2,1,0:T(8,128)(2,1)S(1)}, u32[]{:S(2)}, u32[]{:S(2)}) async-start(bf16[8,3,24,896]{3,2,1,0:T(8,128)(2,1)} %get-tuple-element.71), calls=%async_computation.2 | async-start | bytes 2064384 | tf_op jit(solution)/shard_map/all_to_all | solution.py:332
  157.9 6.6 %shard_map.92 = (bf16[8,5,24,896]{3,2,1,0:T(8,128)(2,1)}, s32[3]{0:T(128)}) custom-call(s32[5]{0:T(128)S(1)} %get-tuple-element.73.place_ref, s32[1]{0:T(128)} %bitcast.1.core_ref, s32[3]{0:T(128)S(1)} %get-tuple-element.69.place_ref.next_ref, bf16[1024,896]{1,0:T(8,128)(2,1)S(1)} %bitcast.47, f32[1,896]{1,0:T(1,128)S(1)} %select_n.79.scales_ref, ...), custom_call_target="tpu_custom_call" | custom-call | tf_op jit(solution)/shard_map/pallas_call | solution.py:137
  164.4 8.1 %all-to-all-done.2.back_ref = bf16[8,3,24,896]{3,2,1,0:T(8,128)(2,1)S(1)} async-done(((bf16[8,3,24,896]{3,2,1,0:T(8,128)(2,1)}), bf16[8,3,24,896]{3,2,1,0:T(8,128)(2,1)S(1)}, u32[]{:S(2)}, u32[]{:S(2)}) %all-to-all-start.2) | async-done | bytes 1032224 | tf_op jit(solution)/shard_map/all_to_all | solution.py:332
  172.5 5.7 %all-to-all-start.3 = ((bf16[8,5,24,896]{3,2,1,0:T(8,128)(2,1)}), bf16[8,5,24,896]{3,2,1,0:T(8,128)(2,1)S(1)}, u32[]{:S(2)}, u32[]{:S(2)}) async-start(bf16[8,5,24,896]{3,2,1,0:T(8,128)(2,1)} %get-tuple-element.75), calls=%async_computation.3 | async-start | bytes 3440640 | tf_op jit(solution)/shard_map/all_to_all | solution.py:335
  178.2 0.1 add_select_fusion
  178.3 0.3 fusion.2
  178.6 1.0 shard_map.93
  179.5 4.0 %collective-permute-start.13 = (bf16[128,896]{1,0:T(8,128)(2,1)}, bf16[128,896]{1,0:T(8,128)(2,1)S(1)}, u32[]{:S(2)}, u32[]{:S(2)}) collective-permute-start(bf16[128,896]{1,0:T(8,128)(2,1)} %get-tuple-element.77), channel_id=1, source_target_pairs={{0,4},{1,5},{2,6},{3,7},{4,0},{5,1},{6,2},{7,3},{8,12},{9,13},{10,... | collective-permute-start | bytes 688136 | tf_op jit(solution)/shard_map/ppermute | solution.py:32
  183.6 1.4 collective-permute-start.14
  185.0 3.7 %collective-permute-start.15 = (bf16[128,896]{1,0:T(8,128)(2,1)S(1)}, bf16[128,896]{1,0:T(8,128)(2,1)S(1)}, u32[]{:S(2)}, u32[]{:S(2)}) collective-permute-start(bf16[128,896]{1,0:T(8,128)(2,1)S(1)} %get-tuple-element.79), channel_id=1, source_target_pairs={{0,5},{1,6},{2,7},{3,0},{4,1},{5,2},{6,3},{7,4},{8,13},{9,14},{10,... | collective-permute-start | bytes 688136 | tf_op jit(solution)/shard_map/ppermute | solution.py:32
  188.6 11.5 %shard_map.94 = f32[896,1024]{1,0:T(8,128)} custom-call(s32[1]{0:T(128)} %bitcast.1.core_ref, bf16[8,2,192,1024]{3,2,1,0:T(8,128)(2,1)} %bitcast.33, bf16[1536,896]{1,0:T(8,128)(2,1)} %bitcast.13.own_ref, bf16[1536,896]{1,0:T(8,128)(2,1)} %collective-permute-done.9.mate_ref), custom_call_target="tpu_custom_call" | custom-call | tf_op jit(solution)/shard_map/pallas_call | solution.py:169
  200.1 2.2 abs_reduce_fusion
  203.0 2.2 collective-permute-start.12
  205.2 4.2 %dynamic-slice_bitcast_fusion = (f32[448,1024]{1,0:T(8,128)}, f16[448,1024]{1,0:T(8,128)(2,1)}) fusion(f32[2,448,1024]{2,1,0:T(8,128)} %bitcast.51, s32[]{:T(128)S(6)} %select_n.84, f32[]{:T(128)} %bitcast.17, s32[]{:T(128)S(6)} %select_n.83), kind=kLoop, calls=%fused_computation.2 | loop fusion | flops 917504 | bytes 6422540 | tf_op jit(solution)/shard_map/jit(dynamic_index_in_dim)/squeeze | solution.py:341
  209.4 0.9 collective-permute-done.14.refs_2_
  210.4 0.9 collective-permute-start.16
  211.3 0.5 shard_map.95
  211.9 0.8 collective-permute-start.17
  212.7 2.4 collective-permute-start.18
  215.1 3.4 %collective-permute-start.19 = (bf16[128,896]{1,0:T(8,128)(2,1)S(1)}, bf16[128,896]{1,0:T(8,128)(2,1)S(1)}, u32[]{:S(2)}, u32[]{:S(2)}) collective-permute-start(bf16[128,896]{1,0:T(8,128)(2,1)S(1)} %get-tuple-element.89), channel_id=1, source_target_pairs={{0,7},{1,0},{2,1},{3,2},{4,3},{5,4},{6,5},{7,6},{8,15},{9,8},{10,9... | collective-permute-start | bytes 688136 | tf_op jit(solution)/shard_map/ppermute | solution.py:32
  218.5 14.1 %collective-permute-done.16 = f16[448,1024]{1,0:T(8,128)(2,1)S(1)} collective-permute-done((f16[448,1024]{1,0:T(8,128)(2,1)}, f16[448,1024]{1,0:T(8,128)(2,1)S(1)}, u32[]{:S(2)}, u32[]{:S(2)}) %collective-permute-start.16) | collective-permute-done | bytes 917536 | tf_op jit(solution)/shard_map/ppermute | solution.py:346
  232.6 2.3 multiply_add_fusion
  234.9 1.8 shard_map.96
  (59 shorter events, 0.9 us)
Async XLA Ops:
  7.2 0.7 copy-start
  7.2 11.3 %copy-start.1 = (bf16[128,7168]{1,0:T(8,128)(2,1)S(1)}, bf16[128,7168]{1,0:T(8,128)(2,1)}, u32[]{:S(2)}) copy-start(bf16[128,7168]{1,0:T(8,128)(2,1)} %hidden_ref.1) | copy-start | bytes 5505028
  8.1 1.0 copy-start.2
  10.9 32.3 %copy-start.8 = (f32[1,448]{1,0:T(1,128)S(1)}, f32[1,448]{1,0:T(1,128)}, u32[]{:S(2)}) copy-start(f32[1,448]{1,0:T(1,128)} %param.10) | copy-start | bytes 5380
  10.9 22.0 %all-to-all-start = ((bf16[16,24,1024]{2,1,0:T(8,128)(2,1)}), bf16[16,24,1024]{2,1,0:T(8,128)(2,1)}, u32[]{:S(2)}, u32[]{:S(2)}) async-start(bf16[16,24,1024]{2,1,0:T(8,128)(2,1)} %bitcast.2), calls=%async_computation | async-start | bytes 1572864 | tf_op jit(solution)/shard_map/all_to_all | solution.py:288
  18.4 115.5 %all-gather.2.cloned.1.call-start = ((), (), s32[]{:S(2)}) async-start(), calls=%async_computation.4 | async-start | bytes 7077888 | tf_op jit(solution)/shard_map/all_gather | solution.py:296
  19.7 0.7 copy-start.3
  20.4 0.7 copy-start.4
  21.1 11.8 %collective-permute-start = (bf16[128,896]{1,0:T(8,128)(2,1)S(1)}, bf16[128,896]{1,0:T(8,128)(2,1)S(1)}, u32[]{:S(2)}, u32[]{:S(2)}) collective-permute-start(bf16[128,896]{1,0:T(8,128)(2,1)S(1)} %get-tuple-element.47), channel_id=1, source_target_pairs={{0,1},{1,2},{2,3},{3,4},{4,5},{5,6},{6,7},{7,0},{8,9},{9,10},{10,1... | collective-permute-start | bytes 688136 | tf_op jit(solution)/shard_map/ppermute | solution.py:32
  23.0 9.9 %collective-permute-start.1 = (bf16[128,896]{1,0:T(8,128)(2,1)S(1)}, bf16[128,896]{1,0:T(8,128)(2,1)S(1)}, u32[]{:S(2)}, u32[]{:S(2)}) collective-permute-start(bf16[128,896]{1,0:T(8,128)(2,1)S(1)} %get-tuple-element.48), channel_id=1, source_target_pairs={{0,7},{1,0},{2,1},{3,2},{4,3},{5,4},{6,5},{7,6},{8,15},{9,8},{10,9... | collective-permute-start | bytes 688136 | tf_op jit(solution)/shard_map/ppermute | solution.py:32
  32.9 39.8 %collective-permute-start.4 = (bf16[128,896]{1,0:T(8,128)(2,1)}, bf16[128,896]{1,0:T(8,128)(2,1)S(1)}, u32[]{:S(2)}, u32[]{:S(2)}) collective-permute-start(bf16[128,896]{1,0:T(8,128)(2,1)} %get-tuple-element.50), channel_id=1, source_target_pairs={{0,4},{1,5},{2,6},{3,7},{4,0},{5,1},{6,2},{7,3},{8,12},{9,13},{10,... | collective-permute-start | bytes 688136 | tf_op jit(solution)/shard_map/ppermute | solution.py:32
  38.5 35.3 %collective-permute-start.5 = (bf16[128,896]{1,0:T(8,128)(2,1)}, bf16[128,896]{1,0:T(8,128)(2,1)S(1)}, u32[]{:S(2)}, u32[]{:S(2)}) collective-permute-start(bf16[128,896]{1,0:T(8,128)(2,1)} %get-tuple-element.51), channel_id=1, source_target_pairs={{0,5},{1,6},{2,7},{3,0},{4,1},{5,2},{6,3},{7,4},{8,13},{9,14},{10,... | collective-permute-start | bytes 688136 | tf_op jit(solution)/shard_map/ppermute | solution.py:32
  38.5 35.3 %collective-permute-start.6 = (bf16[128,896]{1,0:T(8,128)(2,1)}, bf16[128,896]{1,0:T(8,128)(2,1)}, u32[]{:S(2)}, u32[]{:S(2)}) collective-permute-start(bf16[128,896]{1,0:T(8,128)(2,1)} %get-tuple-element.52), channel_id=1, source_target_pairs={{0,3},{1,4},{2,5},{3,6},{4,7},{5,0},{6,1},{7,2},{8,11},{9,12},{10,... | collective-permute-start | bytes 688136 | tf_op jit(solution)/shard_map/ppermute | solution.py:32
  42.3 22.6 %collective-permute-start.2 = (bf16[448,1024]{1,0:T(8,128)(2,1)}, bf16[448,1024]{1,0:T(8,128)(2,1)S(1)}, u32[]{:S(2)}, u32[]{:S(2)}) collective-permute-start(bf16[448,1024]{1,0:T(8,128)(2,1)} %bitcast.54), channel_id=1, source_target_pairs={{0,8},{8,0},{1,9},{9,1},{2,10},{10,2},{3,11},{11,3},{4,12},{12,4},... | collective-permute-start | bytes 2752520 | tf_op jit(solution)/shard_map/ppermute | solution.py:284
  43.2 20.4 %collective-permute-start.3 = (f32[448]{0:T(512)S(1)}, f32[448]{0:T(512)S(1)}, u32[]{:S(2)}, u32[]{:S(2)}) collective-permute-start(f32[448]{0:T(512)S(1)} %bitcast.56), channel_id=1, source_target_pairs={{0,8},{8,0},{1,9},{9,1},{2,10},{10,2},{3,11},{11,3},{4,12},{12,4},... | collective-permute-start | bytes 5384 | tf_op jit(solution)/shard_map/ppermute | solution.py:284
  63.6 19.3 %collective-permute-start.7 = (bf16[128,896]{1,0:T(8,128)(2,1)}, bf16[128,896]{1,0:T(8,128)(2,1)}, u32[]{:S(2)}, u32[]{:S(2)}) collective-permute-start(bf16[128,896]{1,0:T(8,128)(2,1)} %copy-done.4), channel_id=1, source_target_pairs={{0,6},{1,7},{2,0},{3,1},{4,2},{5,3},{6,4},{7,5},{8,14},{9,15},{10,... | collective-permute-start | bytes 688136 | tf_op jit(solution)/shard_map/ppermute | solution.py:32
  64.9 21.9 %collective-permute-start.8 = (bf16[128,896]{1,0:T(8,128)(2,1)}, bf16[128,896]{1,0:T(8,128)(2,1)}, u32[]{:S(2)}, u32[]{:S(2)}) collective-permute-start(bf16[128,896]{1,0:T(8,128)(2,1)} %copy-done.3), channel_id=1, source_target_pairs={{0,2},{1,3},{2,4},{3,5},{4,6},{5,7},{6,0},{7,1},{8,10},{9,11},{10,... | collective-permute-start | bytes 688136 | tf_op jit(solution)/shard_map/ppermute | solution.py:32
  90.4 7.4 %copy-start.10 = (s32[3]{0:T(128)S(1)}, s32[3]{0:T(128)}, u32[]{:S(2)}) copy-start(s32[3]{0:T(128)} %constant.80.clone) | copy-start | bytes 40
  90.4 38.7 %all-to-all-start.1 = ((bf16[8,8,24,896]{3,2,1,0:T(8,128)(2,1)}), bf16[8,8,24,896]{3,2,1,0:T(8,128)(2,1)}, u32[]{:S(2)}, u32[]{:S(2)}) async-start(bf16[8,8,24,896]{3,2,1,0:T(8,128)(2,1)} %shard_map.88), calls=%async_computation.1 | async-start | bytes 5505024 | tf_op jit(solution)/shard_map/all_to_all | solution.py:309
  133.9 8.1 %slice-start = ((s8[6291456]{0:T(1024)(128)(4,1)}), s8[4194304]{0:T(1024)(128)(4,1)S(1)}, s32[]{:S(2)}) async-start(s8[6291456]{0:T(1024)(128)(4,1)} %bitcast.34), calls=%async_computation.5 | async-start | bytes 8388608
  133.9 4.0 %copy-start.9 = (s32[5]{0:T(128)S(1)}, s32[5]{0:T(128)}, u32[]{:S(2)}) copy-start(s32[5]{0:T(128)} %constant.81.clone) | copy-start | bytes 64
  133.9 8.1 %slice-start.1 = ((s8[6291456]{0:T(1024)(128)(4,1)}), s8[2097152]{0:T(1024)(128)(4,1)S(1)}, s32[]{:S(2)}) async-start(s8[6291456]{0:T(1024)(128)(4,1)} %bitcast.34), calls=%async_computation.6 | async-start | bytes 4194304
  137.6 4.4 %collective-permute-start.10 = (f32[576,896]{1,0:T(8,128)S(1)}, f32[576,896]{1,0:T(8,128)S(1)}, u32[]{:S(2)}, u32[]{:S(2)}) collective-permute-start(f32[576,896]{1,0:T(8,128)S(1)} %get-tuple-element.70), channel_id=1, source_target_pairs={{0,16},{16,0},{1,17},{17,1},{2,18},{18,2},{3,19},{19,3},{4,20},{20... | collective-permute-start | bytes 6193160 | tf_op jit(solution)/shard_map/ppermute | solution.py:329
  150.6 7.2 %collective-permute-start.11 = (f32[960,896]{1,0:T(8,128)}, f32[960,896]{1,0:T(8,128)}, u32[]{:S(2)}, u32[]{:S(2)}) collective-permute-start(f32[960,896]{1,0:T(8,128)} %get-tuple-element.74), channel_id=1, source_target_pairs={{0,16},{16,0},{1,17},{17,1},{2,18},{18,2},{3,19},{19,3},{4,20},{20... | collective-permute-start | bytes 10321928 | tf_op jit(solution)/shard_map/ppermute | solution.py:331
  150.9 37.8 %collective-permute-start.9 = (bf16[1536,896]{1,0:T(8,128)(2,1)}, bf16[1536,896]{1,0:T(8,128)(2,1)}, u32[]{:S(2)}, u32[]{:S(2)}) collective-permute-start(bf16[1536,896]{1,0:T(8,128)(2,1)} %bitcast.13.own_ref), channel_id=1, source_target_pairs={{0,16},{16,0},{1,17},{17,1},{2,18},{18,2},{3,19},{19,3},{4,20},{20... | collective-permute-start | bytes 8257544 | tf_op jit(solution)/shard_map/ppermute | solution.py:311
  151.2 21.3 %all-to-all-start.2 = ((bf16[8,3,24,896]{3,2,1,0:T(8,128)(2,1)}), bf16[8,3,24,896]{3,2,1,0:T(8,128)(2,1)S(1)}, u32[]{:S(2)}, u32[]{:S(2)}) async-start(bf16[8,3,24,896]{3,2,1,0:T(8,128)(2,1)} %get-tuple-element.71), calls=%async_computation.2 | async-start | bytes 2064384 | tf_op jit(solution)/shard_map/all_to_all | solution.py:332
  172.5 37.8 %all-to-all-start.3 = ((bf16[8,5,24,896]{3,2,1,0:T(8,128)(2,1)}), bf16[8,5,24,896]{3,2,1,0:T(8,128)(2,1)S(1)}, u32[]{:S(2)}, u32[]{:S(2)}) async-start(bf16[8,5,24,896]{3,2,1,0:T(8,128)(2,1)} %get-tuple-element.75), calls=%async_computation.3 | async-start | bytes 3440640 | tf_op jit(solution)/shard_map/all_to_all | solution.py:335
  178.6 6.4 %copy-start.6 = (bf16[8,8,24,128]{3,2,1,0:T(8,128)(2,1)}, bf16[8,8,24,128]{3,2,1,0:T(8,128)(2,1)S(1)}, u32[]{:S(2)}) copy-start(bf16[8,8,24,128]{3,2,1,0:T(8,128)(2,1)S(1)} %fusion.2) | copy-start | bytes 1179652
  179.5 29.9 %collective-permute-start.13 = (bf16[128,896]{1,0:T(8,128)(2,1)}, bf16[128,896]{1,0:T(8,128)(2,1)S(1)}, u32[]{:S(2)}, u32[]{:S(2)}) collective-permute-start(bf16[128,896]{1,0:T(8,128)(2,1)} %get-tuple-element.77), channel_id=1, source_target_pairs={{0,4},{1,5},{2,6},{3,7},{4,0},{5,1},{6,2},{7,3},{8,12},{9,13},{10,... | collective-permute-start | bytes 688136 | tf_op jit(solution)/shard_map/ppermute | solution.py:32
  183.6 26.8 %collective-permute-start.14 = (bf16[128,896]{1,0:T(8,128)(2,1)S(1)}, bf16[128,896]{1,0:T(8,128)(2,1)S(1)}, u32[]{:S(2)}, u32[]{:S(2)}) collective-permute-start(bf16[128,896]{1,0:T(8,128)(2,1)S(1)} %get-tuple-element.78), channel_id=1, source_target_pairs={{0,3},{1,4},{2,5},{3,6},{4,7},{5,0},{6,1},{7,2},{8,11},{9,12},{10,... | collective-permute-start | bytes 688136 | tf_op jit(solution)/shard_map/ppermute | solution.py:32
  185.0 25.4 %collective-permute-start.15 = (bf16[128,896]{1,0:T(8,128)(2,1)S(1)}, bf16[128,896]{1,0:T(8,128)(2,1)S(1)}, u32[]{:S(2)}, u32[]{:S(2)}) collective-permute-start(bf16[128,896]{1,0:T(8,128)(2,1)S(1)} %get-tuple-element.79), channel_id=1, source_target_pairs={{0,5},{1,6},{2,7},{3,0},{4,1},{5,2},{6,3},{7,4},{8,13},{9,14},{10,... | collective-permute-start | bytes 688136 | tf_op jit(solution)/shard_map/ppermute | solution.py:32
  203.0 7.4 %collective-permute-start.12 = (f32[1]{0:T(128)}, f32[1]{0:T(128)}, u32[]{:S(2)}, u32[]{:S(2)}) collective-permute-start(f32[1]{0:T(128)} %bitcast.16), channel_id=1, source_target_pairs={{0,8},{8,0},{1,9},{9,1},{2,10},{10,2},{3,11},{11,3},{4,12},{12,4},... | collective-permute-start | bytes 20 | tf_op jit(solution)/shard_map/ppermute | solution.py:344
  205.2 6.1 %copy-start.7 = (bf16[8,8,24,128]{3,2,1,0:T(8,128)(2,1)S(1)}, bf16[8,8,24,128]{3,2,1,0:T(8,128)(2,1)}, u32[]{:S(2)}) copy-start(bf16[8,8,24,128]{3,2,1,0:T(8,128)(2,1)} %copy-done.6) | copy-start | bytes 1179652
  210.4 22.2 %copy-start.5 = (f32[448,1024]{1,0:T(8,128)S(1)}, f32[448,1024]{1,0:T(8,128)}, u32[]{:S(2)}) copy-start(f32[448,1024]{1,0:T(8,128)} %get-tuple-element.83) | copy-start | bytes 5505028
  210.4 22.2 %collective-permute-start.16 = (f16[448,1024]{1,0:T(8,128)(2,1)}, f16[448,1024]{1,0:T(8,128)(2,1)S(1)}, u32[]{:S(2)}, u32[]{:S(2)}) collective-permute-start(f16[448,1024]{1,0:T(8,128)(2,1)} %get-tuple-element.84), channel_id=1, source_target_pairs={{0,8},{8,0},{1,9},{9,1},{2,10},{10,2},{3,11},{11,3},{4,12},{12,4},... | collective-permute-start | bytes 2752520 | tf_op jit(solution)/shard_map/ppermute | solution.py:346
  211.9 23.0 %collective-permute-start.17 = (bf16[128,896]{1,0:T(8,128)(2,1)S(1)}, bf16[128,896]{1,0:T(8,128)(2,1)S(1)}, u32[]{:S(2)}, u32[]{:S(2)}) collective-permute-start(bf16[128,896]{1,0:T(8,128)(2,1)S(1)} %get-tuple-element.87), channel_id=1, source_target_pairs={{0,6},{1,7},{2,0},{3,1},{4,2},{5,3},{6,4},{7,5},{8,14},{9,15},{10,... | collective-permute-start | bytes 688136 | tf_op jit(solution)/shard_map/ppermute | solution.py:32
  212.7 22.1 %collective-permute-start.18 = (bf16[128,896]{1,0:T(8,128)(2,1)S(1)}, bf16[128,896]{1,0:T(8,128)(2,1)S(1)}, u32[]{:S(2)}, u32[]{:S(2)}) collective-permute-start(bf16[128,896]{1,0:T(8,128)(2,1)S(1)} %get-tuple-element.88), channel_id=1, source_target_pairs={{0,2},{1,3},{2,4},{3,5},{4,6},{5,7},{6,0},{7,1},{8,10},{9,11},{10,... | collective-permute-start | bytes 688136 | tf_op jit(solution)/shard_map/ppermute | solution.py:32
  215.1 19.7 %collective-permute-start.19 = (bf16[128,896]{1,0:T(8,128)(2,1)S(1)}, bf16[128,896]{1,0:T(8,128)(2,1)S(1)}, u32[]{:S(2)}, u32[]{:S(2)}) collective-permute-start(bf16[128,896]{1,0:T(8,128)(2,1)S(1)} %get-tuple-element.89), channel_id=1, source_target_pairs={{0,7},{1,0},{2,1},{3,2},{4,3},{5,4},{6,5},{7,6},{8,15},{9,8},{10,9... | collective-permute-start | bytes 688136 | tf_op jit(solution)/shard_map/ppermute | solution.py:32
  218.5 16.4 %collective-permute-start.20 = (bf16[128,896]{1,0:T(8,128)(2,1)S(1)}, bf16[128,896]{1,0:T(8,128)(2,1)S(1)}, u32[]{:S(2)}, u32[]{:S(2)}) collective-permute-start(bf16[128,896]{1,0:T(8,128)(2,1)S(1)} %get-tuple-element.90), channel_id=1, source_target_pairs={{0,1},{1,2},{2,3},{3,4},{4,5},{5,6},{6,7},{7,0},{8,9},{9,10},{10,1... | collective-permute-start | bytes 688136 | tf_op jit(solution)/shard_map/ppermute | solution.py:32
Sparse Core Ops, SparseCore 0:
  33.0 100.8 all-gather.1
